TPU v7x, 32 devices: a whole 2x2x4 slice. The times are simulated.
32 devices in a mesh: seq: 8 (over y, x, core), pipe: 4 (over z).
Axes of the slice: x: 2, y: 2, z: 4, core: 2. Of those that a mesh axis runs over, the one named last changes fastest.
Arguments:
- queries: bfloat16 [4, 1024, 12288], P('pipe', 'seq'), may hold values from -5.5 to 5.5
- keys: bfloat16 [4, 1024, 1024], P('pipe', 'seq'), may hold values from -5.5 to 5.5
- values: bfloat16 [4, 1024, 1024], P('pipe', 'seq'), may hold values from -6 to 6
- outputs: bfloat16 [4, 1024, 12288], P('pipe', 'seq'), may hold values from -3 to 3
- incoming: bfloat16 [4, 1024, 12288], P('pipe', 'seq'), may hold values from -6 to 6
- block_mask: int32 [4, 8, 8], P('pipe'), may hold values from 0 to 1, as said below
Outputs:
- grad_queries: bfloat16 [4, 1024, 12288], P('pipe', 'seq')
- grad_keys: bfloat16 [4, 1024, 1024], P('pipe', 'seq')
- grad_values: bfloat16 [4, 1024, 1024], P('pipe', 'seq')
Inputs may be any that keep to these rules, and one draw needn't show every extreme that they name: block_mask[p, i, j] is 1 where query block i and key block j lie in the same passage, or where block i lies in the question, which takes the last 1 to max(1, 2) blocks of section p's sequence; else 0. Passages are runs of whole blocks before the question and differ from section to section.
All inputs are finite; a program needn't handle non-finite values.
Results may differ from a plain program's by a relative error of at most 0.0051.
Values may be sent and summed in bfloat16 or wider, within the bound.
A program may use at most 128 MiB of HBM per device.

v0:
```python
import functools
import math

import jax
import jax.numpy as jnp
from jax import lax
from jax.experimental import pallas as pl
from jax.experimental.pallas import tpu as pltpu
from jax.sharding import PartitionSpec as P

H = 96
KVH = 8
DH = 128
GROUP = H // KVH
WIDE = GROUP * DH
TILE_HEADS = 4
KEY_CHUNK = 256
AHEAD = 3
NEG_FILL = -1e30
MESH = pl.DeviceIdType.MESH
NT = (((1,), (1,)), ((), ()))
NN = (((1,), (0,)), ((), ()))


def dot(a, b, dims):
    return lax.dot_general(a, b, dims, preferred_element_type=jnp.float32)


def kernel(n, pipe, rows, q_hbm, k_hbm, v_hbm, o_hbm, g_hbm, mask_ref, dq_hbm, dk_ref, dv_ref,
           q_buf, o_buf, g_buf, dq_buf, k_buf, v_buf, kt_buf, bias, s_buf, acc_k, acc_v,
           stage, part, own, load_sem, self_sem, dq_sem, g_send, g_recv, kv_send, kv_recv,
           part_send, part_recv):
    me = lax.axis_index("seq")
    section = lax.axis_index("pipe")
    before = lax.rem(section + pipe - 1, pipe)
    after = lax.rem(section + 1, pipe)
    length = n * rows
    scaling = DH ** -0.5
    to_log2 = scaling * math.log2(math.e)

    def cols(c, width):
        return pl.ds(pl.multiple_of(c * width, width), width)

    def block(j):
        return pl.ds(pl.multiple_of(j * rows, rows), rows)

    def g_copy(c):
        return pltpu.make_async_remote_copy(
            src_ref=g_hbm.at[0, :, cols(c, WIDE)], dst_ref=g_buf.at[:, cols(c, WIDE)],
            send_sem=g_send.at[c], recv_sem=g_recv.at[c],
            device_id={"pipe": before}, device_id_type=MESH)

    def kv_copies(c, slot, peer):
        return [
            pltpu.make_async_remote_copy(
                src_ref=hbm.at[0, :, cols(c, DH)], dst_ref=buf.at[c, block(slot), :],
                send_sem=kv_send.at[w, c, peer], recv_sem=kv_recv.at[w, c, slot],
                device_id={"seq": peer}, device_id_type=MESH)
            for w, (hbm, buf) in enumerate(((k_hbm, k_buf), (v_hbm, v_buf)))
        ]

    def part_copy(c, slot, peer):
        return pltpu.make_async_remote_copy(
            src_ref=stage.at[c, block(peer), :], dst_ref=part.at[c, block(slot), :],
            send_sem=part_send.at[c, peer], recv_sem=part_recv.at[c, slot],
            device_id={"seq": peer}, device_id_type=MESH)

    def dq_copy(c):
        return pltpu.make_async_copy(
            dq_buf.at[:, cols(c, WIDE)], dq_hbm.at[0, :, cols(c, WIDE)], dq_sem.at[c])

    def self_copies(c):
        return [
            pltpu.make_async_copy(hbm.at[0, :, cols(c, DH)], buf.at[c, block(me), :], self_sem.at[w, c])
            for w, (hbm, buf) in enumerate(((k_hbm, k_buf), (v_hbm, v_buf)))
        ]

    barrier = pltpu.get_barrier_semaphore()

    def greet(d, carried):
        pl.semaphore_signal(barrier, inc=1, device_id={"seq": lax.rem(me + d, n)}, device_id_type=MESH)
        return carried

    lax.fori_loop(1, n, greet, 0)
    for neighbour in (before, after):
        pl.semaphore_signal(barrier, inc=1, device_id={"pipe": neighbour}, device_id_type=MESH)
    pl.semaphore_wait(barrier, n + 1)

    def send_group(c):
        g_copy(c).start()

        def to_peer(peer, carried):
            for copy in kv_copies(c, me, peer):
                copy.start()
            return carried

        lax.fori_loop(me + 1, n, to_peer, 0)

    q_load = pltpu.make_async_copy(q_hbm.at[0], q_buf, load_sem.at[0])
    o_load = pltpu.make_async_copy(o_hbm.at[0], o_buf, load_sem.at[1])

    def first_sends(c, carried):
        send_group(c)
        return carried

    lax.fori_loop(0, min(AHEAD, KVH), first_sends, 0)
    q_load.start()
    o_load.start()

    def own_block(c, carried):
        for copy in self_copies(c):
            copy.start()
        return carried

    lax.fori_loop(0, KVH, own_block, 0)

    def fill_bias(j, carried):
        k_pos = j * rows + lax.broadcasted_iota(jnp.int32, (rows, rows), 0)
        q_pos = me * rows + lax.broadcasted_iota(jnp.int32, (rows, rows), 1)
        closed = NEG_FILL * (1 - mask_ref[0, me, j]).astype(jnp.float32)
        bias[block(j), :] = jnp.where(k_pos <= q_pos, closed, NEG_FILL)
        return carried

    lax.fori_loop(0, n, fill_bias, 0)

    def clear(j, carried):
        k_buf[:, block(j), :] = jnp.zeros((KVH, rows, DH), jnp.bfloat16)
        v_buf[:, block(j), :] = jnp.zeros((KVH, rows, DH), jnp.bfloat16)
        return carried

    lax.fori_loop(me + 1, n, clear, 0)
    q_load.wait()
    o_load.wait()

    width = TILE_HEADS * rows
    chunks = length // KEY_CHUNK

    def group(c, carried):
        for copy in self_copies(c):
            copy.wait()

        def from_peer(slot, carried):
            for copy in kv_copies(c, slot, slot):
                copy.wait_recv()
            return carried

        lax.fori_loop(0, me, from_peer, 0)
        g_copy(c).wait_recv()

        @pl.when(c + AHEAD < KVH)
        def _():
            send_group(c + AHEAD)

        kt_buf[...] = k_buf[c].T
        acc_k[...] = jnp.zeros_like(acc_k)
        acc_v[...] = jnp.zeros_like(acc_v)

        def tile(t, carried):
            first = c * GROUP + t * TILE_HEADS

            def stacked(buf):
                return jnp.concatenate(
                    [buf[:, cols(first + i, DH)] for i in range(TILE_HEADS)], axis=0)

            q = stacked(q_buf)
            top = None
            for k in range(chunks):
                at = slice(k * KEY_CHUNK, (k + 1) * KEY_CHUNK)
                b = bias[at, :]
                s = dot(k_buf[c, at, :], q, NT) + jnp.concatenate([b] * TILE_HEADS, axis=1)
                s_buf[at, :] = s
                high = jnp.max(s.reshape(KEY_CHUNK // 8, 8, width), axis=0)
                top = high if top is None else jnp.maximum(top, high)
            top = jnp.max(top, axis=0, keepdims=True)
            total = None
            for k in range(chunks):
                at = slice(k * KEY_CHUNK, (k + 1) * KEY_CHUNK)
                p = jnp.exp2((s_buf[at, :] - top) * to_log2)
                s_buf[at, :] = p
                piece = jnp.sum(p.reshape(KEY_CHUNK // 8, 8, width), axis=0)
                total = piece if total is None else total + piece
            inverse = 1.0 / jnp.sum(total, axis=0, keepdims=True)
            g = stacked(g_buf)
            product = stacked(o_buf).astype(jnp.float32) * g.astype(jnp.float32)
            upper = product.astype(jnp.bfloat16)
            lower = (product - upper.astype(jnp.float32)).astype(jnp.bfloat16)
            ones = jnp.ones((8, DH), jnp.bfloat16)
            row_terms = (dot(ones, upper, NT) + dot(ones, lower, NT))[0:1]
            dqt = None
            for k in range(chunks):
                at = slice(k * KEY_CHUNK, (k + 1) * KEY_CHUNK)
                weights = s_buf[at, :] * inverse
                dw = dot(v_buf[c, at, :], g, NT)
                dl = (weights * (dw - row_terms)).astype(jnp.bfloat16)
                acc_v[at, :] += dot(weights.astype(jnp.bfloat16), g, NN)
                acc_k[at, :] += dot(dl, q, NN)
                piece = dot(kt_buf[:, at], dl, NN)
                dqt = piece if dqt is None else dqt + piece
            for i in range(TILE_HEADS):
                one = dqt[:, i * rows:(i + 1) * rows].T * scaling
                dq_buf[:, cols(first + i, DH)] = one.astype(jnp.bfloat16)
            return carried

        lax.fori_loop(0, GROUP // TILE_HEADS, tile, 0)
        dq_copy(c).start()
        stage[c, :, 0:DH] = (acc_k[...] * scaling).astype(jnp.bfloat16)
        stage[c, :, DH:2 * DH] = acc_v[...].astype(jnp.bfloat16)
        own[c, :, 0:DH] = acc_k[block(me), :] * scaling
        own[c, :, DH:2 * DH] = acc_v[block(me), :]

        def to_owner(peer, carried):
            part_copy(c, me, peer).start()
            return carried

        lax.fori_loop(0, me, to_owner, 0)
        return carried

    lax.fori_loop(0, KVH, group, 0)

    def finish(c, carried):
        def take(slot, total):
            part_copy(c, slot, slot).wait_recv()
            return total + part[c, block(slot), :].astype(jnp.float32)

        total = lax.fori_loop(me + 1, n, take, own[c]).astype(jnp.bfloat16)
        dk_ref[0, :, cols(c, DH)] = total[:, 0:DH]
        dv_ref[0, :, cols(c, DH)] = total[:, DH:2 * DH]
        return carried

    lax.fori_loop(0, KVH, finish, 0)

    def settle(c, carried):
        g_copy(c).wait_send()
        dq_copy(c).wait()

        def sent_kv(peer, carried):
            for copy in kv_copies(c, me, peer):
                copy.wait_send()
            return carried

        lax.fori_loop(me + 1, n, sent_kv, 0)

        def sent_part(peer, carried):
            part_copy(c, me, peer).wait_send()
            return carried

        lax.fori_loop(0, me, sent_part, 0)
        return carried

    lax.fori_loop(0, KVH, settle, 0)


def on_device(queries, keys, values, outputs, incoming, block_mask):
    n = lax.axis_size("seq")
    pipe = lax.axis_size("pipe")
    rows = queries.shape[1]
    length = n * rows
    anywhere = pl.BlockSpec(memory_space=pl.ANY)
    vmem = pl.BlockSpec(memory_space=pltpu.VMEM)
    low = jnp.bfloat16
    full = jnp.float32
    return pl.pallas_call(
        functools.partial(kernel, n, pipe, rows),
        out_shape=(
            jax.ShapeDtypeStruct(queries.shape, low),
            jax.ShapeDtypeStruct(keys.shape, low),
            jax.ShapeDtypeStruct(values.shape, low),
        ),
        in_specs=[anywhere] * 5 + [pl.BlockSpec(memory_space=pltpu.SMEM)],
        out_specs=(anywhere, vmem, vmem),
        scratch_shapes=[
            pltpu.VMEM((rows, H * DH), low),
            pltpu.VMEM((rows, H * DH), low),
            pltpu.VMEM((rows, H * DH), low),
            pltpu.VMEM((rows, H * DH), low),
            pltpu.VMEM((KVH, length, DH), low),
            pltpu.VMEM((KVH, length, DH), low),
            pltpu.VMEM((DH, length), low),
            pltpu.VMEM((length, rows), full),
            pltpu.VMEM((length, TILE_HEADS * rows), full),
            pltpu.VMEM((length, DH), full),
            pltpu.VMEM((length, DH), full),
            pltpu.VMEM((KVH, length, 2 * DH), low),
            pltpu.VMEM((KVH, length, 2 * DH), low),
            pltpu.VMEM((KVH, rows, 2 * DH), full),
            pltpu.SemaphoreType.DMA((2,)),
            pltpu.SemaphoreType.DMA((2, KVH)),
            pltpu.SemaphoreType.DMA((KVH,)),
            pltpu.SemaphoreType.DMA((KVH,)),
            pltpu.SemaphoreType.DMA((KVH,)),
            pltpu.SemaphoreType.DMA((2, KVH, n)),
            pltpu.SemaphoreType.DMA((2, KVH, n)),
            pltpu.SemaphoreType.DMA((KVH, n)),
            pltpu.SemaphoreType.DMA((KVH, n)),
        ],
        compiler_params=pltpu.CompilerParams(
            collective_id=0, has_side_effects=True, vmem_limit_bytes=58 * 1024 * 1024),
        cost_estimate=pl.CostEstimate(
            flops=10 * rows * length * H * DH,
            bytes_accessed=5 * rows * H * DH * 2,
            transcendentals=rows * length * H),
    )(queries, keys, values, outputs, incoming, block_mask)


def solution(mesh):
    placed = (
        P("pipe", "seq", None),
        P("pipe", "seq", None),
        P("pipe", "seq", None),
        P("pipe", "seq", None),
        P("pipe", "seq", None),
        P("pipe", None, None),
    )
    return jax.shard_map(
        on_device,
        mesh=mesh,
        in_specs=placed,
        out_specs=(P("pipe", "seq", None), P("pipe", "seq", None), P("pipe", "seq", None)),
        check_vma=False,
    )
```

profile of v0, /device:TPU:1, one launch (start us, length us, event | category | flops | bytes accessed | tf_op | source)
XLA Modules:
  0.0 98.0 jit_solution(15644732501323694791)
XLA Ops:
  0.6 92.1 %shard_map.85 = (bf16[1,128,12288]{2,1,0:T(8,128)(2,1)}, bf16[1,128,1024]{2,1,0:T(8,128)(2,1)}, bf16[1,128,1024]{2,1,0:T(8,128)(2,1)}) custom-call(bf16[1,128,12288]{2,1,0:T(8,128)(2,1)} %q_hbm.1, bf16[1,128,1024]{2,1,0:T(8,128)(2,1)} %k_hbm.1, bf16[1,128,1024]{2,1,0:T(8,128)(2,1)} %v_hbm.1, bf16[1,128,12288]{2,1,0:T(8,128)(2,1)} %o_hbm.1, ...), custom_call_target="tpu_custom_call" | custom-call | flops 16106127360 | bytes 15728640 | tf_op jit(solution)/shard_map/pallas_call | solution.py:262
  92.7 0.0 copy-start.1
  92.7 0.0 copy-start
  92.7 3.9 %copy.12 = bf16[1,128,12288]{2,1,0:T(8,128)(2,1)} copy(bf16[1,128,12288]{2,1,0:T(8,128)(2,1)} %get-tuple-element.6) | data formatting | bytes 6291456
  96.6 0.0 copy-done.1
  96.6 0.7 copy.13
  97.3 0.0 copy-done
  97.3 0.7 copy.14
Async XLA Ops:
  92.7 3.9 %copy-start.1 = (bf16[1,128,1024]{2,1,0:T(8,128)(2,1)S(1)}, bf16[1,128,1024]{2,1,0:T(8,128)(2,1)}, u32[]{:S(2)}) copy-start(bf16[1,128,1024]{2,1,0:T(8,128)(2,1)} %get-tuple-element.7) | copy-start | bytes 786436
  92.7 4.6 %copy-start = (bf16[1,128,1024]{2,1,0:T(8,128)(2,1)S(1)}, bf16[1,128,1024]{2,1,0:T(8,128)(2,1)}, u32[]{:S(2)}) copy-start(bf16[1,128,1024]{2,1,0:T(8,128)(2,1)} %get-tuple-element.8) | copy-start | bytes 786436
where the time goes:
time: 98.2 us; the launch traced here: 98 us
  Pallas kernels  92.1 us (94%)
  local copies, waits for them, and re-layouts  5.3 us (5%)
    pallas_call x1, Pallas kernels, on_device(): pl.pallas_call(functools.partial(kernel, n, pipe, rows), out_shape=(jax.S...  92.1 us
    unnamed x7, local copies, waits for them, and re-layouts  5.3 us

commit v1 on v0

--- a/solution.py
+++ b/solution.py
@@ -15,7 +15,11 @@
 WIDE = GROUP * DH
 TILE_HEADS = 4
 KEY_CHUNK = 256
-AHEAD = 3
+TILES = GROUP // TILE_HEADS
+CHUNK = TILE_HEADS * DH
+PARTS = KVH * TILES
+KV_AHEAD = 2
+G_AHEAD = 6
 NEG_FILL = -1e30
 MESH = pl.DeviceIdType.MESH
 NT = (((1,), (1,)), ((), ()))
@@ -26,9 +30,9 @@
     return lax.dot_general(a, b, dims, preferred_element_type=jnp.float32)
 
 
-def kernel(n, pipe, rows, q_hbm, k_hbm, v_hbm, o_hbm, g_hbm, mask_ref, dq_hbm, dk_ref, dv_ref,
-           q_buf, o_buf, g_buf, dq_buf, k_buf, v_buf, kt_buf, bias, s_buf, acc_k, acc_v,
-           stage, part, own, load_sem, self_sem, dq_sem, g_send, g_recv, kv_send, kv_recv,
+def kernel(n, pipe, rows, q_hbm, k_hbm, v_hbm, o_hbm, g_hbm, mask_hbm, dq_ref, dk_ref, dv_ref,
+           mask_ref, q_buf, o_buf, g_buf, k_buf, v_buf, kt_buf, bias, s_buf, acc_k, acc_v,
+           stage, part, own, load_sem, self_sem, g_send, g_recv, kv_send, kv_recv,
            part_send, part_recv):
     me = lax.axis_index("seq")
     section = lax.axis_index("pipe")
@@ -46,7 +50,7 @@
 
     def g_copy(c):
         return pltpu.make_async_remote_copy(
-            src_ref=g_hbm.at[0, :, cols(c, WIDE)], dst_ref=g_buf.at[:, cols(c, WIDE)],
+            src_ref=g_hbm.at[0, :, cols(c, CHUNK)], dst_ref=g_buf.at[:, cols(c, CHUNK)],
             send_sem=g_send.at[c], recv_sem=g_recv.at[c],
             device_id={"pipe": before}, device_id_type=MESH)
 
@@ -65,10 +69,6 @@
             send_sem=part_send.at[c, peer], recv_sem=part_recv.at[c, slot],
             device_id={"seq": peer}, device_id_type=MESH)
 
-    def dq_copy(c):
-        return pltpu.make_async_copy(
-            dq_buf.at[:, cols(c, WIDE)], dq_hbm.at[0, :, cols(c, WIDE)], dq_sem.at[c])
-
     def self_copies(c):
         return [
             pltpu.make_async_copy(hbm.at[0, :, cols(c, DH)], buf.at[c, block(me), :], self_sem.at[w, c])
@@ -86,9 +86,7 @@
         pl.semaphore_signal(barrier, inc=1, device_id={"pipe": neighbour}, device_id_type=MESH)
     pl.semaphore_wait(barrier, n + 1)
 
-    def send_group(c):
-        g_copy(c).start()
-
+    def send_keys(c):
         def to_peer(peer, carried):
             for copy in kv_copies(c, me, peer):
                 copy.start()
@@ -96,14 +94,18 @@
 
         lax.fori_loop(me + 1, n, to_peer, 0)
 
+    def send_grads(c, carried):
+        g_copy(c).start()
+        return carried
+
+    mask_load = pltpu.make_async_copy(mask_hbm, mask_ref, load_sem.at[2])
+    mask_load.start()
     q_load = pltpu.make_async_copy(q_hbm.at[0], q_buf, load_sem.at[0])
     o_load = pltpu.make_async_copy(o_hbm.at[0], o_buf, load_sem.at[1])
 
-    def first_sends(c, carried):
-        send_group(c)
-        return carried
-
-    lax.fori_loop(0, min(AHEAD, KVH), first_sends, 0)
+    lax.fori_loop(0, G_AHEAD, send_grads, 0)
+    for c in range(KV_AHEAD):
+        send_keys(c)
     q_load.start()
     o_load.start()
 
@@ -121,6 +123,7 @@
         bias[block(j), :] = jnp.where(k_pos <= q_pos, closed, NEG_FILL)
         return carried
 
+    mask_load.wait()
     lax.fori_loop(0, n, fill_bias, 0)
 
     def clear(j, carried):
@@ -135,6 +138,15 @@
     width = TILE_HEADS * rows
     chunks = length // KEY_CHUNK
 
+    def finish(c):
+        def take(slot, total):
+            part_copy(c, slot, slot).wait_recv()
+            return total + part[c, block(slot), :].astype(jnp.float32)
+
+        total = lax.fori_loop(me + 1, n, take, own[c]).astype(jnp.bfloat16)
+        dk_ref[0, :, cols(c, DH)] = total[:, 0:DH]
+        dv_ref[0, :, cols(c, DH)] = total[:, DH:2 * DH]
+
     def group(c, carried):
         for copy in self_copies(c):
             copy.wait()
@@ -145,11 +157,14 @@
             return carried
 
         lax.fori_loop(0, me, from_peer, 0)
-        g_copy(c).wait_recv()
-
-        @pl.when(c + AHEAD < KVH)
+
+        @pl.when(c + KV_AHEAD < KVH)
         def _():
-            send_group(c + AHEAD)
+            send_keys(c + KV_AHEAD)
+
+        @pl.when(c >= 2)
+        def _():
+            finish(c - 2)
 
         kt_buf[...] = k_buf[c].T
         acc_k[...] = jnp.zeros_like(acc_k)
@@ -180,6 +195,13 @@
                 piece = jnp.sum(p.reshape(KEY_CHUNK // 8, 8, width), axis=0)
                 total = piece if total is None else total + piece
             inverse = 1.0 / jnp.sum(total, axis=0, keepdims=True)
+            now = c * TILES + t
+            g_copy(now).wait_recv()
+
+            @pl.when(now + G_AHEAD < PARTS)
+            def _():
+                g_copy(now + G_AHEAD).start()
+
             g = stacked(g_buf)
             product = stacked(o_buf).astype(jnp.float32) * g.astype(jnp.float32)
             upper = product.astype(jnp.bfloat16)
@@ -198,11 +220,10 @@
                 dqt = piece if dqt is None else dqt + piece
             for i in range(TILE_HEADS):
                 one = dqt[:, i * rows:(i + 1) * rows].T * scaling
-                dq_buf[:, cols(first + i, DH)] = one.astype(jnp.bfloat16)
-            return carried
-
-        lax.fori_loop(0, GROUP // TILE_HEADS, tile, 0)
-        dq_copy(c).start()
+                dq_ref[0, :, cols(first + i, DH)] = one.astype(jnp.bfloat16)
+            return carried
+
+        lax.fori_loop(0, TILES, tile, 0)
         stage[c, :, 0:DH] = (acc_k[...] * scaling).astype(jnp.bfloat16)
         stage[c, :, DH:2 * DH] = acc_v[...].astype(jnp.bfloat16)
         own[c, :, 0:DH] = acc_k[block(me), :] * scaling
@@ -217,22 +238,10 @@
 
     lax.fori_loop(0, KVH, group, 0)
 
-    def finish(c, carried):
-        def take(slot, total):
-            part_copy(c, slot, slot).wait_recv()
-            return total + part[c, block(slot), :].astype(jnp.float32)
-
-        total = lax.fori_loop(me + 1, n, take, own[c]).astype(jnp.bfloat16)
-        dk_ref[0, :, cols(c, DH)] = total[:, 0:DH]
-        dv_ref[0, :, cols(c, DH)] = total[:, DH:2 * DH]
-        return carried
-
-    lax.fori_loop(0, KVH, finish, 0)
+    finish(KVH - 2)
+    finish(KVH - 1)
 
     def settle(c, carried):
-        g_copy(c).wait_send()
-        dq_copy(c).wait()
-
         def sent_kv(peer, carried):
             for copy in kv_copies(c, me, peer):
                 copy.wait_send()
@@ -248,6 +257,24 @@
         return carried
 
     lax.fori_loop(0, KVH, settle, 0)
+
+    def sent_grads(c, carried):
+        g_copy(c).wait_send()
+        return carried
+
+    lax.fori_loop(0, PARTS, sent_grads, 0)
+
+
+def write_out(*refs):
+    sources, targets, sems = refs[0:3], refs[3:6], refs[6]
+    copies = [
+        pltpu.make_async_copy(source, target, sems.at[w])
+        for w, (source, target) in enumerate(zip(sources, targets))
+    ]
+    for copy in copies:
+        copy.start()
+    for copy in copies:
+        copy.wait()
 
 
 def on_device(queries, keys, values, outputs, incoming, block_mask):
@@ -255,21 +282,20 @@
     pipe = lax.axis_size("pipe")
     rows = queries.shape[1]
     length = n * rows
-    anywhere = pl.BlockSpec(memory_space=pl.ANY)
     vmem = pl.BlockSpec(memory_space=pltpu.VMEM)
     low = jnp.bfloat16
     full = jnp.float32
-    return pl.pallas_call(
+    grads = pl.pallas_call(
         functools.partial(kernel, n, pipe, rows),
         out_shape=(
-            jax.ShapeDtypeStruct(queries.shape, low),
-            jax.ShapeDtypeStruct(keys.shape, low),
-            jax.ShapeDtypeStruct(values.shape, low),
+            pltpu.VMEM(queries.shape, low),
+            pltpu.VMEM(keys.shape, low),
+            pltpu.VMEM(values.shape, low),
         ),
-        in_specs=[anywhere] * 5 + [pl.BlockSpec(memory_space=pltpu.SMEM)],
-        out_specs=(anywhere, vmem, vmem),
+        in_specs=[pl.BlockSpec(memory_space=pltpu.HBM)] * 6,
+        out_specs=(vmem, vmem, vmem),
         scratch_shapes=[
-            pltpu.VMEM((rows, H * DH), low),
+            pltpu.SMEM(block_mask.shape, jnp.int32),
             pltpu.VMEM((rows, H * DH), low),
             pltpu.VMEM((rows, H * DH), low),
             pltpu.VMEM((rows, H * DH), low),
@@ -283,23 +309,30 @@
             pltpu.VMEM((KVH, length, 2 * DH), low),
             pltpu.VMEM((KVH, length, 2 * DH), low),
             pltpu.VMEM((KVH, rows, 2 * DH), full),
-            pltpu.SemaphoreType.DMA((2,)),
+            pltpu.SemaphoreType.DMA((3,)),
             pltpu.SemaphoreType.DMA((2, KVH)),
-            pltpu.SemaphoreType.DMA((KVH,)),
-            pltpu.SemaphoreType.DMA((KVH,)),
-            pltpu.SemaphoreType.DMA((KVH,)),
+            pltpu.SemaphoreType.DMA((PARTS,)),
+            pltpu.SemaphoreType.DMA((PARTS,)),
             pltpu.SemaphoreType.DMA((2, KVH, n)),
             pltpu.SemaphoreType.DMA((2, KVH, n)),
             pltpu.SemaphoreType.DMA((KVH, n)),
             pltpu.SemaphoreType.DMA((KVH, n)),
         ],
         compiler_params=pltpu.CompilerParams(
-            collective_id=0, has_side_effects=True, vmem_limit_bytes=58 * 1024 * 1024),
+            collective_id=0, has_side_effects=True, vmem_limit_bytes=52 * 1024 * 1024),
         cost_estimate=pl.CostEstimate(
             flops=10 * rows * length * H * DH,
             bytes_accessed=5 * rows * H * DH * 2,
             transcendentals=rows * length * H),
     )(queries, keys, values, outputs, incoming, block_mask)
+    return pl.pallas_call(
+        write_out,
+        out_shape=[jax.ShapeDtypeStruct(grad.shape, low) for grad in grads],
+        in_specs=[vmem] * 3,
+        out_specs=[pl.BlockSpec(memory_space=pltpu.HBM)] * 3,
+        scratch_shapes=[pltpu.SemaphoreType.DMA((3,))],
+        compiler_params=pltpu.CompilerParams(vmem_limit_bytes=1024 * 1024),
+    )(*grads)
 
 
 def solution(mesh):

time: 98.2 us -> 88.9 us (0.905)
  local copies, waits for them, and re-layouts: 5.3 us -> 0 us
  Pallas kernels: 92.1 us -> 88.1 us
    unnamed x7 -> x0, local copies, waits for them, and re-layouts: 5.3 us -> none
    pallas_call x1 -> x2, Pallas kernels: 92.1 us -> 88.1 us  [the longest x1 86.3 us: on_device(): pl.pallas_call(functools.partial(kernel, n, pipe, rows), out_shape=(pltpu...]
where the time goes in v1:
time: 88.9 us; the launch traced here: 88.7 us
  Pallas kernels  88.1 us (99%)
    pallas_call x1, Pallas kernels, on_device(): pl.pallas_call(functools.partial(kernel, n, pipe, rows), out_shape=(pltpu...  86.3 us
    pallas_call x1, Pallas kernels, on_device(): pl.pallas_call(write_out, out_shape=[jax.ShapeDtypeStruct(grad.shape, low...  1.85 us

profile of v1, /device:TPU:1, one launch (start us, length us, event | category | flops | bytes accessed | tf_op | source)
XLA Modules:
  0.0 88.7 jit_solution(13346206353809402387)
XLA Ops:
  0.6 86.3 %shard_map.85 = (bf16[1,128,12288]{2,1,0:T(8,128)(2,1)S(1)}, bf16[1,128,1024]{2,1,0:T(8,128)(2,1)S(1)}, bf16[1,128,1024]{2,1,0:T(8,128)(2,1)S(1)}) custom-call(bf16[1,128,12288]{2,1,0:T(8,128)(2,1)} %q_hbm.1, bf16[1,128,1024]{2,1,0:T(8,128)(2,1)} %k_hbm.1, bf16[1,128,1024]{2,1,0:T(8,128)(2,1)} %v_hbm.1, bf16[1,128,12288]{2,1,0:T(8,128)(2,1)} %o_hbm.1, ...), custom_call_target="tpu_custom_call" | custom-call | flops 16106127360 | bytes 15728640 | tf_op jit(solution)/shard_map/pallas_call | solution.py:288
  86.9 1.9 %shard_map.86 = (bf16[1,128,12288]{2,1,0:T(8,128)(2,1)}, bf16[1,128,1024]{2,1,0:T(8,128)(2,1)}, bf16[1,128,1024]{2,1,0:T(8,128)(2,1)}) custom-call(bf16[1,128,12288]{2,1,0:T(8,128)(2,1)S(1)} %get-tuple-element.6.refs_0_, bf16[1,128,1024]{2,1,0:T(8,128)(2,1)S(1)} %get-tuple-element.7.refs_1_, bf16[1,128,1024]{2,1,0:T(8,128)(2,1)S(1)} %get-tuple-element.8.refs_2_), custom_call_target="tpu_custom_call" | custom-call | tf_op jit(solution)/shard_map/pallas_call | solution.py:328

commit v2 on v1

--- a/solution.py
+++ b/solution.py
@@ -170,7 +170,11 @@
         acc_k[...] = jnp.zeros_like(acc_k)
         acc_v[...] = jnp.zeros_like(acc_v)
 
-        def tile(t, carried):
+        def to_owner(peer, carried):
+            part_copy(c, me, peer).start()
+            return carried
+
+        def tile(t, carried, last=False):
             first = c * GROUP + t * TILE_HEADS
 
             def stacked(buf):
@@ -218,22 +222,23 @@
                 acc_k[at, :] += dot(dl, q, NN)
                 piece = dot(kt_buf[:, at], dl, NN)
                 dqt = piece if dqt is None else dqt + piece
+                if last:
+                    stage[c, at, 0:DH] = (acc_k[at, :] * scaling).astype(jnp.bfloat16)
+                    stage[c, at, DH:2 * DH] = acc_v[at, :].astype(jnp.bfloat16)
+                    if k == chunks // 2 - 1:
+                        lax.fori_loop(0, jnp.minimum(me, n // 2), to_owner, 0)
+            if last:
+                lax.fori_loop(n // 2, me, to_owner, 0)
             for i in range(TILE_HEADS):
                 one = dqt[:, i * rows:(i + 1) * rows].T * scaling
                 dq_ref[0, :, cols(first + i, DH)] = one.astype(jnp.bfloat16)
             return carried
 
-        lax.fori_loop(0, TILES, tile, 0)
-        stage[c, :, 0:DH] = (acc_k[...] * scaling).astype(jnp.bfloat16)
-        stage[c, :, DH:2 * DH] = acc_v[...].astype(jnp.bfloat16)
+        lax.fori_loop(0, TILES - 1, tile, 0)
+        tile(TILES - 1, 0, True)
         own[c, :, 0:DH] = acc_k[block(me), :] * scaling
         own[c, :, DH:2 * DH] = acc_v[block(me), :]
 
-        def to_owner(peer, carried):
-            part_copy(c, me, peer).start()
-            return carried
-
-        lax.fori_loop(0, me, to_owner, 0)
         return carried
 
     lax.fori_loop(0, KVH, group, 0)

time: 88.9 us -> 88.2 us (level)
  no operation moved by 1% of the time
where the time goes in v2:
time: 88.2 us; the launch traced here: 88 us
  Pallas kernels  87.4 us (99%)
    pallas_call x1, Pallas kernels, on_device(): pl.pallas_call(functools.partial(kernel, n, pipe, rows), out_shape=(pltpu...  85.5 us
    pallas_call x1, Pallas kernels, on_device(): pl.pallas_call(write_out, out_shape=[jax.ShapeDtypeStruct(grad.shape, low...  1.85 us

profile of v2, /device:TPU:1, one launch (start us, length us, event | category | flops | bytes accessed | tf_op | source)
XLA Modules:
  0.0 88.0 jit_solution(7207891742675233265)
XLA Ops:
  0.6 85.5 %shard_map.85 = (bf16[1,128,12288]{2,1,0:T(8,128)(2,1)S(1)}, bf16[1,128,1024]{2,1,0:T(8,128)(2,1)S(1)}, bf16[1,128,1024]{2,1,0:T(8,128)(2,1)S(1)}) custom-call(bf16[1,128,12288]{2,1,0:T(8,128)(2,1)} %q_hbm.1, bf16[1,128,1024]{2,1,0:T(8,128)(2,1)} %k_hbm.1, bf16[1,128,1024]{2,1,0:T(8,128)(2,1)} %v_hbm.1, bf16[1,128,12288]{2,1,0:T(8,128)(2,1)} %o_hbm.1, ...), custom_call_target="tpu_custom_call" | custom-call | flops 16106127360 | bytes 15728640 | tf_op jit(solution)/shard_map/pallas_call | solution.py:293
  86.1 1.9 %shard_map.86 = (bf16[1,128,12288]{2,1,0:T(8,128)(2,1)}, bf16[1,128,1024]{2,1,0:T(8,128)(2,1)}, bf16[1,128,1024]{2,1,0:T(8,128)(2,1)}) custom-call(bf16[1,128,12288]{2,1,0:T(8,128)(2,1)S(1)} %get-tuple-element.6.refs_0_, bf16[1,128,1024]{2,1,0:T(8,128)(2,1)S(1)} %get-tuple-element.7.refs_1_, bf16[1,128,1024]{2,1,0:T(8,128)(2,1)S(1)} %get-tuple-element.8.refs_2_), custom_call_target="tpu_custom_call" | custom-call | tf_op jit(solution)/shard_map/pallas_call | solution.py:333
